TPU v7x, 128 devices: a whole 4x4x4 slice. The times are simulated.
128 devices in a mesh: dom: 32 (over x, z, core), grp: 4 (over y).
Axes of the slice: x: 4, y: 4, z: 4, core: 2. Of those that a mesh axis runs over, the one named last changes fastest.
Arguments:
- x_current: bfloat16 [524288, 128], P(('dom', 'grp')), may hold values from -6 to 6
- x_cached: bfloat16 [524288, 128], P(('dom', 'grp')), may hold values from -6 to 6
- w_self: bfloat16 [128, 512], replicated, may hold values from -0.5 to 0.5
- w_neigh: bfloat16 [128, 512], replicated, may hold values from -1 to 1
- bias: float32 [512], replicated, may hold values from -3 to 3
- tile_columns: int32 [4096, 40], P(('dom', 'grp')), may hold values from 0 to 255
- tile_count: int32 [4096], P(('dom', 'grp')), may hold values from 1 to 40, as said below
- adjacency: int32 [4096, 40, 2048], P(('dom', 'grp')), may hold values from 0 to 255, as said below
- degree: int32 [524288], P(('dom', 'grp')), may hold values from 1 to 5128, as said below
- boundary_blocks: int32 [128, 1], P(('dom', 'grp')), may hold values from 0 to 31
Outputs:
- hidden: bfloat16 [524288, 512], P(('dom', 'grp'))
Inputs may be any that keep to these rules, and one draw needn't show every extreme that they name: `tile_count`: every device has a row block with all 40 slots live. `adjacency`: 8 entries of a tile row packed into each word, bit b for column 8 c + b. `degree`: at least the number of ones in the row of the live tiles of the node's row block.
All inputs are finite; a program needn't handle non-finite values.
Results may differ from a plain program's by a relative error of at most 0.0025.
Values may be sent and summed in bfloat16 or wider, within the bound.
A program may use at most 192 MiB of HBM per device.

v0:
```python
import math
import jax
import jax.numpy as jnp
from jax import lax
from jax.sharding import PartitionSpec as P


def on_device(
    x_current,
    x_cached,
    w_self,
    w_neigh,
    bias,
    tile_columns,
    tile_count,
    adjacency,
    degree,
    boundary_blocks,
):
    node_rows, width = x_current.shape
    row_blocks, per_tile = tile_columns.shape
    tile_rows = node_rows // row_blocks
    chosen = x_cached.reshape(row_blocks, tile_rows, width)[boundary_blocks[0]]
    received = lax.all_gather(x_current, "grp", axis=0, tiled=True)
    part_blocks = received.reshape(-1, tile_rows, width)
    partial_value = lax.all_gather(chosen[None, None], "grp", axis=1, tiled=True)
    halo_blocks = lax.all_gather(partial_value, "dom", axis=0, tiled=True)
    block_table = jnp.concatenate([part_blocks, halo_blocks.reshape(-1, tile_rows, width)], axis=0)
    group_size = math.gcd(4, row_blocks)
    turns = row_blocks // group_size
    shifts = jnp.arange(8, dtype=jnp.int32)

    def one_group(pieces):
        columns, counts, packed = pieces
        bit_values = (
            packed.reshape(group_size, per_tile, tile_rows, tile_rows // 8, 1) >> shifts & 1
        )
        live_mask = (jnp.arange(per_tile, dtype=jnp.int32)[None, :] < counts[:, None]).astype(
            jnp.int32
        )
        adjacent = (
            bit_values.reshape(group_size, per_tile, tile_rows, tile_rows)
            * live_mask[:, :, None, None]
        ).astype(jnp.bfloat16)
        gathered = block_table[columns]
        return jnp.einsum("stij,stjf->sif", adjacent, gathered, preferred_element_type=jnp.float32)

    totals = lax.map(
        one_group,
        (
            tile_columns.reshape(turns, group_size, per_tile),
            tile_count.reshape(turns, group_size),
            adjacency.reshape(turns, group_size, per_tile, -1),
        ),
    )
    totals = totals.reshape(node_rows, width)
    average = (totals / degree.astype(jnp.float32)[:, None]).astype(jnp.bfloat16)
    summed = (
        jnp.dot(x_current, w_self, preferred_element_type=jnp.float32)
        + jnp.dot(average, w_neigh, preferred_element_type=jnp.float32)
        + bias
    )
    return jnp.maximum(summed, 0.0).astype(jnp.bfloat16)


def solution(mesh):
    in_specs = (
        P(("dom", "grp"), None),
        P(("dom", "grp"), None),
        P(),
        P(),
        P(),
        P(("dom", "grp"), None),
        P(("dom", "grp")),
        P(("dom", "grp"), None, None),
        P(("dom", "grp")),
        P(("dom", "grp"), None),
    )
    out_specs = P(("dom", "grp"), None)
    return jax.shard_map(
        on_device, mesh=mesh, in_specs=in_specs, out_specs=out_specs, check_vma=False
    )
```

profile of v0, /device:TPU:1, one launch (start us, length us, event | category | flops | bytes accessed | tf_op | source)
XLA Modules:
  0.0 343.1 jit_solution(17156375614477139263)
XLA Ops:
  8.0 11.2 %all-gather = bf16[4,128,128]{2,1,0:T(8,128)(2,1)} all-gather(bf16[1,128,128]{2,1,0:T(8,128)(2,1)S(1)} %constant_dynamic-slice_fusion.2), channel_id=2, replica_groups=mesh['dom'=32,'grp'=4] {'grp'}, dimensions={0}, use_global_device_ids=true | all-gather | bytes 163840 | tf_op jit(solution)/shard_map/all_gather | solution.py:26
  19.3 20.7 %copy.16 = s32[32,40,2048]{1,2,0:T(8,128)} copy(s32[32,40,2048]{2,1,0:T(8,128)} %param.19) | data formatting | bytes 20971520 | tf_op args[7]
  40.1 4.4 %fusion.21 = f32[4096,512]{1,0:T(8,128)} fusion(bf16[4096,128]{1,0:T(8,128)(2,1)S(1)} %copy-done.2, bf16[128,512]{1,0:T(8,128)(2,1)S(1)} %copy-done.3), kind=kOutput, calls=%fused_computation.26 | convolution fusion | flops 536870912 | bytes 9568256 | tf_op jit(solution)/shard_map/dot_general | solution.py:59
  44.5 16.1 %all-gather.5.cloned.1.call-done = bf16[16384,128]{1,0:T(8,128)(2,1)} async-done(((bf16[4096,128]{1,0:T(8,128)(2,1)}), bf16[16384,128]{1,0:T(8,128)(2,1)}) %all-gather.5.cloned.1.call-update) | async-done | bytes 4194320 | tf_op jit(solution)/shard_map/all_gather | solution.py:24
  60.6 49.4 %all-gather.7.cloned.1.call-done = bf16[128,128,128]{2,1,0:T(8,128)(2,1)} async-done(((bf16[4,128,128]{2,1,0:T(8,128)(2,1)}), bf16[128,128,128]{2,1,0:T(8,128)(2,1)}) %all-gather.7.cloned.1.call-update) | async-done | bytes 4194320 | tf_op jit(solution)/shard_map/all_gather | solution.py:27
  110.0 7.4 %pad_maximum_fusion = bf16[256,128,128]{2,1,0:T(8,128)(2,1)} fusion(bf16[128,128,128]{2,1,0:T(8,128)(2,1)} %all-gather.7.cloned.1.call-done, bf16[128,128,128]{2,1,0:T(8,128)(2,1)} %bitcast.63), kind=kLoop, calls=%fused_computation.21 | loop fusion | flops 4194304 | bytes 16777216 | tf_op jit(solution)/shard_map/concatenate | solution.py:28
  117.4 210.2 %while.12 = (s32[]{:T(128)}, f32[8,4,128,128]{3,2,1,0:T(8,128)}, s32[8,4,40,2048]{2,3,1,0:T(8,128)}, s32[8,4]{1,0:T(8,128)S(1)}, s32[8,4,40]{2,1,0:T(4,128)}, /*index=5*/bf16[256,128,128]{2,1,0:T(8,128)(2,1)}, s32[]{:T(128)}) while((s32[]{:T(128)}, f32[8,4,128,128]{3,2,1,0:T(8,128)}, s32[8,4,40,2048]{2,3,1,0:T(8,128)}, ...), condition=%wide.region_1.2_spmd.clone, body=%wide.region_0.1_spmd.clone.sunk | while | flops 681576256 | bytes 22556296 | solution.py:48
  118.2 11.2 %gather_fusion = bf16[160,128,128]{2,1,0:T(8,128)(2,1)} fusion(bf16[256,128,128]{2,1,0:T(8,128)(2,1)} %get-tuple-element.136, s32[1024]{0:T(1024)S(1)} %pad_clamp_fusion.2), kind=kCustom, calls=%fused_computation.clone.clone.1 | custom fusion | bytes 10486400 | tf_op jit(solution)/shard_map/while/body/eval_jaxpr/gather | solution.py:45
  129.3 4.5 %constant_dynamic-slice_fusion.4 = s32[1,4,40,2048]{2,3,1,0:T(8,128)} fusion(s32[8,4,40,2048]{2,3,1,0:T(8,128)} %get-tuple-element.133, s32[]{:T(128)} %get-tuple-element.124), kind=kLoop, calls=%fused_computation.18.clone.1 | loop fusion | bytes 2621444 | tf_op jit(solution)/shard_map/while/body/jit(dynamic_index_in_dim)/dynamic_slice | solution.py:48
  137.4 6.3 %fusion.36 = f32[8,4,128,128]{3,2,1,0:T(8,128)} fusion(f32[8,4,128,128]{3,2,1,0:T(8,128)} %get-tuple-element.125, s32[]{:T(128)} %get-tuple-element.124, bf16[4,40,128,128]{3,2,1,0:T(8,128)(2,1)} %bitcast.61, s32[4,40]{1,0:T(4,128)S(1)} %fusion.35, s32[128]{0:T(128)S(1)} %shift_right_arithmetic.64, s32[4,40,128,16]{2,3,1,0:T(8,128)S(1)} %copy.20), kind=kOutput, calls=%fused_computation.12.clone.1 | convolution fusion | flops 681574400 | bytes 6817408 | tf_op jit(solution)/shard_map/while/body/eval_jaxpr/stij,stjf->sif/dot_general | solution.py:46
  144.4 11.2 %gather_fusion = bf16[160,128,128]{2,1,0:T(8,128)(2,1)} fusion(bf16[256,128,128]{2,1,0:T(8,128)(2,1)} %get-tuple-element.136, s32[1024]{0:T(1024)S(1)} %pad_clamp_fusion.2), kind=kCustom, calls=%fused_computation.clone.clone.1 | custom fusion | bytes 10486400 | tf_op jit(solution)/shard_map/while/body/eval_jaxpr/gather | solution.py:45
  155.6 4.5 %constant_dynamic-slice_fusion.4 = s32[1,4,40,2048]{2,3,1,0:T(8,128)} fusion(s32[8,4,40,2048]{2,3,1,0:T(8,128)} %get-tuple-element.133, s32[]{:T(128)} %get-tuple-element.124), kind=kLoop, calls=%fused_computation.18.clone.1 | loop fusion | bytes 2621444 | tf_op jit(solution)/shard_map/while/body/jit(dynamic_index_in_dim)/dynamic_slice | solution.py:48
  163.7 6.3 %fusion.36 = f32[8,4,128,128]{3,2,1,0:T(8,128)} fusion(f32[8,4,128,128]{3,2,1,0:T(8,128)} %get-tuple-element.125, s32[]{:T(128)} %get-tuple-element.124, bf16[4,40,128,128]{3,2,1,0:T(8,128)(2,1)} %bitcast.61, s32[4,40]{1,0:T(4,128)S(1)} %fusion.35, s32[128]{0:T(128)S(1)} %shift_right_arithmetic.64, s32[4,40,128,16]{2,3,1,0:T(8,128)S(1)} %copy.20), kind=kOutput, calls=%fused_computation.12.clone.1 | convolution fusion | flops 681574400 | bytes 6817408 | tf_op jit(solution)/shard_map/while/body/eval_jaxpr/stij,stjf->sif/dot_general | solution.py:46
  170.7 11.2 %gather_fusion = bf16[160,128,128]{2,1,0:T(8,128)(2,1)} fusion(bf16[256,128,128]{2,1,0:T(8,128)(2,1)} %get-tuple-element.136, s32[1024]{0:T(1024)S(1)} %pad_clamp_fusion.2), kind=kCustom, calls=%fused_computation.clone.clone.1 | custom fusion | bytes 10486400 | tf_op jit(solution)/shard_map/while/body/eval_jaxpr/gather | solution.py:45
  181.9 4.5 %constant_dynamic-slice_fusion.4 = s32[1,4,40,2048]{2,3,1,0:T(8,128)} fusion(s32[8,4,40,2048]{2,3,1,0:T(8,128)} %get-tuple-element.133, s32[]{:T(128)} %get-tuple-element.124), kind=kLoop, calls=%fused_computation.18.clone.1 | loop fusion | bytes 2621444 | tf_op jit(solution)/shard_map/while/body/jit(dynamic_index_in_dim)/dynamic_slice | solution.py:48
  189.9 6.3 %fusion.36 = f32[8,4,128,128]{3,2,1,0:T(8,128)} fusion(f32[8,4,128,128]{3,2,1,0:T(8,128)} %get-tuple-element.125, s32[]{:T(128)} %get-tuple-element.124, bf16[4,40,128,128]{3,2,1,0:T(8,128)(2,1)} %bitcast.61, s32[4,40]{1,0:T(4,128)S(1)} %fusion.35, s32[128]{0:T(128)S(1)} %shift_right_arithmetic.64, s32[4,40,128,16]{2,3,1,0:T(8,128)S(1)} %copy.20), kind=kOutput, calls=%fused_computation.12.clone.1 | convolution fusion | flops 681574400 | bytes 6817408 | tf_op jit(solution)/shard_map/while/body/eval_jaxpr/stij,stjf->sif/dot_general | solution.py:46
  197.0 11.2 %gather_fusion = bf16[160,128,128]{2,1,0:T(8,128)(2,1)} fusion(bf16[256,128,128]{2,1,0:T(8,128)(2,1)} %get-tuple-element.136, s32[1024]{0:T(1024)S(1)} %pad_clamp_fusion.2), kind=kCustom, calls=%fused_computation.clone.clone.1 | custom fusion | bytes 10486400 | tf_op jit(solution)/shard_map/while/body/eval_jaxpr/gather | solution.py:45
  208.1 4.5 %constant_dynamic-slice_fusion.4 = s32[1,4,40,2048]{2,3,1,0:T(8,128)} fusion(s32[8,4,40,2048]{2,3,1,0:T(8,128)} %get-tuple-element.133, s32[]{:T(128)} %get-tuple-element.124), kind=kLoop, calls=%fused_computation.18.clone.1 | loop fusion | bytes 2621444 | tf_op jit(solution)/shard_map/while/body/jit(dynamic_index_in_dim)/dynamic_slice | solution.py:48
  216.2 6.3 %fusion.36 = f32[8,4,128,128]{3,2,1,0:T(8,128)} fusion(f32[8,4,128,128]{3,2,1,0:T(8,128)} %get-tuple-element.125, s32[]{:T(128)} %get-tuple-element.124, bf16[4,40,128,128]{3,2,1,0:T(8,128)(2,1)} %bitcast.61, s32[4,40]{1,0:T(4,128)S(1)} %fusion.35, s32[128]{0:T(128)S(1)} %shift_right_arithmetic.64, s32[4,40,128,16]{2,3,1,0:T(8,128)S(1)} %copy.20), kind=kOutput, calls=%fused_computation.12.clone.1 | convolution fusion | flops 681574400 | bytes 6817408 | tf_op jit(solution)/shard_map/while/body/eval_jaxpr/stij,stjf->sif/dot_general | solution.py:46
  223.2 11.2 %gather_fusion = bf16[160,128,128]{2,1,0:T(8,128)(2,1)} fusion(bf16[256,128,128]{2,1,0:T(8,128)(2,1)} %get-tuple-element.136, s32[1024]{0:T(1024)S(1)} %pad_clamp_fusion.2), kind=kCustom, calls=%fused_computation.clone.clone.1 | custom fusion | bytes 10486400 | tf_op jit(solution)/shard_map/while/body/eval_jaxpr/gather | solution.py:45
  234.4 4.5 %constant_dynamic-slice_fusion.4 = s32[1,4,40,2048]{2,3,1,0:T(8,128)} fusion(s32[8,4,40,2048]{2,3,1,0:T(8,128)} %get-tuple-element.133, s32[]{:T(128)} %get-tuple-element.124), kind=kLoop, calls=%fused_computation.18.clone.1 | loop fusion | bytes 2621444 | tf_op jit(solution)/shard_map/while/body/jit(dynamic_index_in_dim)/dynamic_slice | solution.py:48
  242.4 6.3 %fusion.36 = f32[8,4,128,128]{3,2,1,0:T(8,128)} fusion(f32[8,4,128,128]{3,2,1,0:T(8,128)} %get-tuple-element.125, s32[]{:T(128)} %get-tuple-element.124, bf16[4,40,128,128]{3,2,1,0:T(8,128)(2,1)} %bitcast.61, s32[4,40]{1,0:T(4,128)S(1)} %fusion.35, s32[128]{0:T(128)S(1)} %shift_right_arithmetic.64, s32[4,40,128,16]{2,3,1,0:T(8,128)S(1)} %copy.20), kind=kOutput, calls=%fused_computation.12.clone.1 | convolution fusion | flops 681574400 | bytes 6817408 | tf_op jit(solution)/shard_map/while/body/eval_jaxpr/stij,stjf->sif/dot_general | solution.py:46
  249.5 11.2 %gather_fusion = bf16[160,128,128]{2,1,0:T(8,128)(2,1)} fusion(bf16[256,128,128]{2,1,0:T(8,128)(2,1)} %get-tuple-element.136, s32[1024]{0:T(1024)S(1)} %pad_clamp_fusion.2), kind=kCustom, calls=%fused_computation.clone.clone.1 | custom fusion | bytes 10486400 | tf_op jit(solution)/shard_map/while/body/eval_jaxpr/gather | solution.py:45
  260.7 4.5 %constant_dynamic-slice_fusion.4 = s32[1,4,40,2048]{2,3,1,0:T(8,128)} fusion(s32[8,4,40,2048]{2,3,1,0:T(8,128)} %get-tuple-element.133, s32[]{:T(128)} %get-tuple-element.124), kind=kLoop, calls=%fused_computation.18.clone.1 | loop fusion | bytes 2621444 | tf_op jit(solution)/shard_map/while/body/jit(dynamic_index_in_dim)/dynamic_slice | solution.py:48
  268.7 6.3 %fusion.36 = f32[8,4,128,128]{3,2,1,0:T(8,128)} fusion(f32[8,4,128,128]{3,2,1,0:T(8,128)} %get-tuple-element.125, s32[]{:T(128)} %get-tuple-element.124, bf16[4,40,128,128]{3,2,1,0:T(8,128)(2,1)} %bitcast.61, s32[4,40]{1,0:T(4,128)S(1)} %fusion.35, s32[128]{0:T(128)S(1)} %shift_right_arithmetic.64, s32[4,40,128,16]{2,3,1,0:T(8,128)S(1)} %copy.20), kind=kOutput, calls=%fused_computation.12.clone.1 | convolution fusion | flops 681574400 | bytes 6817408 | tf_op jit(solution)/shard_map/while/body/eval_jaxpr/stij,stjf->sif/dot_general | solution.py:46
  275.8 11.2 %gather_fusion = bf16[160,128,128]{2,1,0:T(8,128)(2,1)} fusion(bf16[256,128,128]{2,1,0:T(8,128)(2,1)} %get-tuple-element.136, s32[1024]{0:T(1024)S(1)} %pad_clamp_fusion.2), kind=kCustom, calls=%fused_computation.clone.clone.1 | custom fusion | bytes 10486400 | tf_op jit(solution)/shard_map/while/body/eval_jaxpr/gather | solution.py:45
  286.9 4.5 %constant_dynamic-slice_fusion.4 = s32[1,4,40,2048]{2,3,1,0:T(8,128)} fusion(s32[8,4,40,2048]{2,3,1,0:T(8,128)} %get-tuple-element.133, s32[]{:T(128)} %get-tuple-element.124), kind=kLoop, calls=%fused_computation.18.clone.1 | loop fusion | bytes 2621444 | tf_op jit(solution)/shard_map/while/body/jit(dynamic_index_in_dim)/dynamic_slice | solution.py:48
  295.0 6.3 %fusion.36 = f32[8,4,128,128]{3,2,1,0:T(8,128)} fusion(f32[8,4,128,128]{3,2,1,0:T(8,128)} %get-tuple-element.125, s32[]{:T(128)} %get-tuple-element.124, bf16[4,40,128,128]{3,2,1,0:T(8,128)(2,1)} %bitcast.61, s32[4,40]{1,0:T(4,128)S(1)} %fusion.35, s32[128]{0:T(128)S(1)} %shift_right_arithmetic.64, s32[4,40,128,16]{2,3,1,0:T(8,128)S(1)} %copy.20), kind=kOutput, calls=%fused_computation.12.clone.1 | convolution fusion | flops 681574400 | bytes 6817408 | tf_op jit(solution)/shard_map/while/body/eval_jaxpr/stij,stjf->sif/dot_general | solution.py:46
  302.1 11.2 %gather_fusion = bf16[160,128,128]{2,1,0:T(8,128)(2,1)} fusion(bf16[256,128,128]{2,1,0:T(8,128)(2,1)} %get-tuple-element.136, s32[1024]{0:T(1024)S(1)} %pad_clamp_fusion.2), kind=kCustom, calls=%fused_computation.clone.clone.1 | custom fusion | bytes 10486400 | tf_op jit(solution)/shard_map/while/body/eval_jaxpr/gather | solution.py:45
  313.2 4.5 %constant_dynamic-slice_fusion.4 = s32[1,4,40,2048]{2,3,1,0:T(8,128)} fusion(s32[8,4,40,2048]{2,3,1,0:T(8,128)} %get-tuple-element.133, s32[]{:T(128)} %get-tuple-element.124), kind=kLoop, calls=%fused_computation.18.clone.1 | loop fusion | bytes 2621444 | tf_op jit(solution)/shard_map/while/body/jit(dynamic_index_in_dim)/dynamic_slice | solution.py:48
  321.3 6.3 %fusion.36 = f32[8,4,128,128]{3,2,1,0:T(8,128)} fusion(f32[8,4,128,128]{3,2,1,0:T(8,128)} %get-tuple-element.125, s32[]{:T(128)} %get-tuple-element.124, bf16[4,40,128,128]{3,2,1,0:T(8,128)(2,1)} %bitcast.61, s32[4,40]{1,0:T(4,128)S(1)} %fusion.35, s32[128]{0:T(128)S(1)} %shift_right_arithmetic.64, s32[4,40,128,16]{2,3,1,0:T(8,128)S(1)} %copy.20), kind=kOutput, calls=%fused_computation.12.clone.1 | convolution fusion | flops 681574400 | bytes 6817408 | tf_op jit(solution)/shard_map/while/body/eval_jaxpr/stij,stjf->sif/dot_general | solution.py:46
  329.6 6.6 %maximum_convert_fusion = bf16[4096,512]{1,0:T(8,128)(2,1)} fusion(f32[4096,512]{1,0:T(8,128)} %fusion.21, bf16[4096,128]{1,0:T(8,128)(2,1)S(1)} %fusion.20, bf16[128,512]{1,0:T(8,128)(2,1)S(1)} %copy-done.4, f32[512]{0:T(512)S(1)} %copy-done.6), kind=kOutput, calls=%fused_computation.22 | convolution fusion | flops 545259520 | bytes 13764608 | tf_op jit(solution)/shard_map/dot_general | solution.py:60
  (89 shorter events, 37.7 us)
Async XLA Ops:
  6.5 1.4 copy-start
  6.5 54.0 %all-gather.5.cloned.1.call-start = ((), (), s32[]{:S(2)}) async-start(), calls=%async_computation | async-start | bytes 5242880 | tf_op jit(solution)/shard_map/all_gather | solution.py:24
  7.3 102.7 %all-gather.7.cloned.1.call-start = ((), (), s32[]{:S(2)}) async-start(), calls=%async_computation.1 | async-start | bytes 4325376 | tf_op jit(solution)/shard_map/all_gather | solution.py:27
  19.2 20.7 %copy-start.7 = (s32[32]{0:T(128)S(1)}, s32[32]{0:T(128)}, u32[]{:S(2)}) copy-start(s32[32]{0:T(128)} %param.18) | copy-start | bytes 388
  19.2 20.8 %copy-start.5 = (s32[4096]{0:T(1024)S(1)}, s32[4096]{0:T(1024)}, u32[]{:S(2)}) copy-start(s32[4096]{0:T(1024)} %param.20) | copy-start | bytes 49156
  19.2 20.8 %copy-start.2 = (bf16[4096,128]{1,0:T(8,128)(2,1)S(1)}, bf16[4096,128]{1,0:T(8,128)(2,1)}, u32[]{:S(2)}) copy-start(bf16[4096,128]{1,0:T(8,128)(2,1)} %param.12) | copy-start | bytes 3145732
  19.2 20.8 %copy-start.3 = (bf16[128,512]{1,0:T(8,128)(2,1)S(1)}, bf16[128,512]{1,0:T(8,128)(2,1)}, u32[]{:S(2)}) copy-start(bf16[128,512]{1,0:T(8,128)(2,1)} %param.14) | copy-start | bytes 393220
  117.4 212.2 %copy-start.4 = (bf16[128,512]{1,0:T(8,128)(2,1)S(1)}, bf16[128,512]{1,0:T(8,128)(2,1)}, u32[]{:S(2)}) copy-start(bf16[128,512]{1,0:T(8,128)(2,1)} %param.15) | copy-start | bytes 393220
  117.4 212.2 %copy-start.6 = (f32[512]{0:T(512)S(1)}, f32[512]{0:T(512)}, u32[]{:S(2)}) copy-start(f32[512]{0:T(512)} %param.16) | copy-start | bytes 6148
  327.5 8.7 %copy-start.1 = (bf16[4096,128]{1,0:T(8,128)(2,1)S(1)}, bf16[4096,128]{1,0:T(8,128)(2,1)}, u32[]{:S(2)}) copy-start(bf16[4096,128]{1,0:T(8,128)(2,1)} %param.13) | copy-start | bytes 3145732
Sparse Core Ops, SparseCore 0:
  9.0 51.4 all-gather.4
  62.8 47.1 all-gather.6
where the time goes:
time: 345 us; the launch traced here: 343 us
  local copies, waits for them, and re-layouts  174 us (50%)
  waiting for transfers between devices  66.2 us (19%)
  matrix products  61.2 us (18%)
  other arithmetic  15.6 us (5%)
  between operations  14.2 us (4%)
  blocking collectives  11.2 us (3%)
    gather x8, local copies, waits for them, and re-layouts, one_group(): gathered = block_table[columns]  89.3 us
    dot_general x8, matrix products, one_group(): jnp.einsum('stij,stjf->sif', adjacent, gathered, preferred_element_type=j...  50.2 us
    all_gather x1, waiting for transfers between devices, on_device(): halo_blocks = lax.all_gather(partial_value, 'dom', axis=0, tiled=True)  49.4 us
    dynamic_slice x8, local copies, waits for them, and re-layouts, on_device(): lax.map(one_group, (tile_columns.reshape(turns, group_size, per_tile), ti...  35.8 us
    shift_right_arithmetic x24, local copies, waits for them, and re-layouts, one_group(): packed.reshape(group_size, per_tile, tile_rows, tile_rows // 8, 1) >> shifts  27.9 us
    unnamed x17, local copies, waits for them, and re-layouts  20.7 us
    all_gather x1, waiting for transfers between devices, on_device(): received = lax.all_gather(x_current, 'grp', axis=0, tiled=True)  16.1 us
    all_gather x1, blocking collectives, on_device(): lax.all_gather(chosen[None, None], 'grp', axis=1, tiled=True)  11.2 us
  transfers between devices with their start and end apart: 2, of which 2 were waited for; matrix products, arithmetic and copies ran while one was open for 7% of the time, Pallas kernels for 0%

commit v1 on v0

--- a/solution.py
+++ b/solution.py
@@ -21,7 +21,14 @@
     row_blocks, per_tile = tile_columns.shape
     tile_rows = node_rows // row_blocks
     chosen = x_cached.reshape(row_blocks, tile_rows, width)[boundary_blocks[0]]
-    received = lax.all_gather(x_current, "grp", axis=0, tiled=True)
+    ways, here, step = (lax.axis_size("grp"), lax.axis_index("grp"), x_current.shape[0])
+    line, have = (x_current, 1)
+    while have < ways:
+        line = jnp.concatenate(
+            [line, lax.ppermute(line, "grp", [(d, (d - have) % ways) for d in range(ways)])], axis=0
+        )
+        have = 2 * have
+    received = jnp.roll(line, here * step, axis=0)
     part_blocks = received.reshape(-1, tile_rows, width)
     partial_value = lax.all_gather(chosen[None, None], "grp", axis=1, tiled=True)
     halo_blocks = lax.all_gather(partial_value, "dom", axis=0, tiled=True)

time: 345 us -> 331 us (0.959)
  waiting for transfers between devices: 66.2 us -> 19.1 us
  blocking collectives: 11.2 us -> 27.4 us
  local copies, waits for them, and re-layouts: 174 us -> 181 us
  starting transfers between devices: 0.04 us -> 4.91 us
    all_gather x1, waiting for transfers between devices: 49.4 us -> 0.01 us  [on_device(): halo_blocks = lax.all_gather(partial_value, 'dom', axis=0, tiled=True)]
    ppermute x0 -> x2, waiting for transfers between devices: none -> 19.1 us  [on_device(): lax.ppermute(line, 'grp', [(d, (d - have) % ways) for d in range(ways)])]
    all_gather x1, blocking collectives: 11.2 us -> 27.4 us  [on_device(): lax.all_gather(chosen[None, None], 'grp', axis=1, tiled=True)]
    all_gather x1 -> x0, waiting for transfers between devices: 16.1 us -> none  [on_device(): received = lax.all_gather(x_current, 'grp', axis=0, tiled=True)]
    ppermute x0 -> x2, starting transfers between devices: none -> 4.91 us  [on_device(): lax.ppermute(line, 'grp', [(d, (d - have) % ways) for d in range(ways)])]
    unnamed x17 -> x22, local copies, waits for them, and re-layouts: 20.7 us -> 22.8 us
  transfers between devices with their start and end apart: 2 -> 3, of which waited for: 2 -> 1; matrix products, arithmetic and copies ran while one was open for 7% -> 10% of each run, Pallas kernels for 0% -> 0%
where the time goes in v1:
time: 331 us; the launch traced here: 326 us
  local copies, waits for them, and re-layouts  181 us (55%)
  matrix products  61.1 us (18%)
  blocking collectives  27.4 us (8%)
  waiting for transfers between devices  19.1 us (6%)
  other arithmetic  18.3 us (6%)
  between operations  14.2 us (4%)
  starting transfers between devices  4.91 us (1%)
    gather x8, local copies, waits for them, and re-layouts, one_group(): gathered = block_table[columns]  89.3 us
    dot_general x8, matrix products, one_group(): jnp.einsum('stij,stjf->sif', adjacent, gathered, preferred_element_type=j...  50.1 us
    dynamic_slice x8, local copies, waits for them, and re-layouts, on_device(): lax.map(one_group, (tile_columns.reshape(turns, group_size, per_tile), ti...  35.8 us
    shift_right_arithmetic x24, local copies, waits for them, and re-layouts, one_group(): packed.reshape(group_size, per_tile, tile_rows, tile_rows // 8, 1) >> shifts  27.9 us
    all_gather x1, blocking collectives, on_device(): lax.all_gather(chosen[None, None], 'grp', axis=1, tiled=True)  27.4 us
    unnamed x22, local copies, waits for them, and re-layouts  22.8 us
    ppermute x2, waiting for transfers between devices, on_device(): lax.ppermute(line, 'grp', [(d, (d - have) % ways) for d in range(ways)])  19.1 us
    concatenate x1, other arithmetic, on_device(): jnp.concatenate([part_blocks, halo_blocks.reshape(-1, tile_rows, width)],...  7.4 us
  transfers between devices with their start and end apart: 3, of which 1 were waited for; matrix products, arithmetic and copies ran while one was open for 10% of the time, Pallas kernels for 0%

profile of v1, /device:TPU:1, one launch (start us, length us, event | category | flops | bytes accessed | tf_op | source)
XLA Modules:
  0.0 325.8 jit_solution(9039781989333468663)
XLA Ops:
  6.5 3.6 %collective-permute-start = (bf16[4096,128]{1,0:T(8,128)(2,1)}, bf16[4096,128]{1,0:T(8,128)(2,1)S(1)}, u32[]{:S(2)}, u32[]{:S(2)}) collective-permute-start(bf16[4096,128]{1,0:T(8,128)(2,1)} %param.12), channel_id=1, source_target_pairs={{0,3},{1,0},{2,1},{3,2},{4,7},{5,4},{6,5},{7,6},{8,11},{9,8},{10,9... | collective-permute-start | bytes 3145736 | tf_op jit(solution)/shard_map/ppermute | solution.py:28
  10.8 27.4 %all-gather = bf16[4,128,128]{2,1,0:T(8,128)(2,1)} all-gather(bf16[1,128,128]{2,1,0:T(8,128)(2,1)S(1)} %constant_dynamic-slice_fusion.2), channel_id=2, replica_groups=mesh['dom'=32,'grp'=4] {'grp'}, dimensions={0}, use_global_device_ids=true | all-gather | bytes 163840 | tf_op jit(solution)/shard_map/all_gather | solution.py:33
  42.3 20.4 %copy.16 = s32[32,40,2048]{1,2,0:T(8,128)} copy(s32[32,40,2048]{2,1,0:T(8,128)} %param.19) | data formatting | bytes 20971520 | tf_op args[7]
  62.8 4.4 %fusion.21 = f32[4096,512]{1,0:T(8,128)} fusion(bf16[4096,128]{1,0:T(8,128)(2,1)S(1)} %copy-done.2, bf16[128,512]{1,0:T(8,128)(2,1)S(1)} %copy-done.3), kind=kOutput, calls=%fused_computation.34 | convolution fusion | flops 536870912 | bytes 9568256 | tf_op jit(solution)/shard_map/dot_general | solution.py:66
  67.5 19.1 %collective-permute-done.1 = bf16[8192,128]{1,0:T(8,128)(2,1)} collective-permute-done((bf16[8192,128]{1,0:T(8,128)(2,1)}, bf16[8192,128]{1,0:T(8,128)(2,1)}, u32[]{:S(2)}, u32[]{:S(2)}) %collective-permute-start.1) | collective-permute-done | bytes 2097184 | tf_op jit(solution)/shard_map/ppermute | solution.py:28
  92.8 7.4 %pad_maximum_fusion = bf16[256,128,128]{2,1,0:T(8,128)(2,1)} fusion(bf16[128,128,128]{2,1,0:T(8,128)(2,1)} %all-gather.4.cloned.1.call-done, bf16[128,128,128]{2,1,0:T(8,128)(2,1)} %bitcast.63), kind=kLoop, calls=%fused_computation.21 | loop fusion | flops 4194304 | bytes 16777216 | tf_op jit(solution)/shard_map/concatenate | solution.py:35
  100.2 210.1 %while.12 = (s32[]{:T(128)}, f32[8,4,128,128]{3,2,1,0:T(8,128)}, s32[8,4,40,2048]{2,3,1,0:T(8,128)}, s32[8,4]{1,0:T(8,128)S(1)}, s32[8,4,40]{2,1,0:T(4,128)}, /*index=5*/bf16[256,128,128]{2,1,0:T(8,128)(2,1)}, s32[]{:T(128)}) while((s32[]{:T(128)}, f32[8,4,128,128]{3,2,1,0:T(8,128)}, s32[8,4,40,2048]{2,3,1,0:T(8,128)}, ...), condition=%wide.region_1.2_spmd.clone, body=%wide.region_0.1_spmd.clone.sunk | while | flops 681576256 | bytes 22556296 | solution.py:55
  101.0 11.2 %gather_fusion = bf16[160,128,128]{2,1,0:T(8,128)(2,1)} fusion(bf16[256,128,128]{2,1,0:T(8,128)(2,1)} %get-tuple-element.136, s32[1024]{0:T(1024)S(1)} %pad_clamp_fusion.2), kind=kCustom, calls=%fused_computation.clone.clone.1 | custom fusion | bytes 10486400 | tf_op jit(solution)/shard_map/while/body/eval_jaxpr/gather | solution.py:52
  112.1 4.5 %constant_dynamic-slice_fusion.5 = s32[1,4,40,2048]{2,3,1,0:T(8,128)} fusion(s32[8,4,40,2048]{2,3,1,0:T(8,128)} %get-tuple-element.133, s32[]{:T(128)} %get-tuple-element.124), kind=kLoop, calls=%fused_computation.18.clone.1 | loop fusion | bytes 2621444 | tf_op jit(solution)/shard_map/while/body/jit(dynamic_index_in_dim)/dynamic_slice | solution.py:55
  120.2 6.2 %fusion.36 = f32[8,4,128,128]{3,2,1,0:T(8,128)} fusion(f32[8,4,128,128]{3,2,1,0:T(8,128)} %get-tuple-element.125, s32[]{:T(128)} %get-tuple-element.124, bf16[4,40,128,128]{3,2,1,0:T(8,128)(2,1)} %bitcast.61, s32[4,40]{1,0:T(4,128)S(1)} %fusion.35, s32[128]{0:T(128)S(1)} %shift_right_arithmetic.64, s32[4,40,128,16]{2,3,1,0:T(8,128)S(1)} %copy.20), kind=kOutput, calls=%fused_computation.12.clone.1 | convolution fusion | flops 681574400 | bytes 6817408 | tf_op jit(solution)/shard_map/while/body/eval_jaxpr/stij,stjf->sif/dot_general | solution.py:53
  127.2 11.2 %gather_fusion = bf16[160,128,128]{2,1,0:T(8,128)(2,1)} fusion(bf16[256,128,128]{2,1,0:T(8,128)(2,1)} %get-tuple-element.136, s32[1024]{0:T(1024)S(1)} %pad_clamp_fusion.2), kind=kCustom, calls=%fused_computation.clone.clone.1 | custom fusion | bytes 10486400 | tf_op jit(solution)/shard_map/while/body/eval_jaxpr/gather | solution.py:52
  138.4 4.5 %constant_dynamic-slice_fusion.5 = s32[1,4,40,2048]{2,3,1,0:T(8,128)} fusion(s32[8,4,40,2048]{2,3,1,0:T(8,128)} %get-tuple-element.133, s32[]{:T(128)} %get-tuple-element.124), kind=kLoop, calls=%fused_computation.18.clone.1 | loop fusion | bytes 2621444 | tf_op jit(solution)/shard_map/while/body/jit(dynamic_index_in_dim)/dynamic_slice | solution.py:55
  146.4 6.3 %fusion.36 = f32[8,4,128,128]{3,2,1,0:T(8,128)} fusion(f32[8,4,128,128]{3,2,1,0:T(8,128)} %get-tuple-element.125, s32[]{:T(128)} %get-tuple-element.124, bf16[4,40,128,128]{3,2,1,0:T(8,128)(2,1)} %bitcast.61, s32[4,40]{1,0:T(4,128)S(1)} %fusion.35, s32[128]{0:T(128)S(1)} %shift_right_arithmetic.64, s32[4,40,128,16]{2,3,1,0:T(8,128)S(1)} %copy.20), kind=kOutput, calls=%fused_computation.12.clone.1 | convolution fusion | flops 681574400 | bytes 6817408 | tf_op jit(solution)/shard_map/while/body/eval_jaxpr/stij,stjf->sif/dot_general | solution.py:53
  153.5 11.2 %gather_fusion = bf16[160,128,128]{2,1,0:T(8,128)(2,1)} fusion(bf16[256,128,128]{2,1,0:T(8,128)(2,1)} %get-tuple-element.136, s32[1024]{0:T(1024)S(1)} %pad_clamp_fusion.2), kind=kCustom, calls=%fused_computation.clone.clone.1 | custom fusion | bytes 10486400 | tf_op jit(solution)/shard_map/while/body/eval_jaxpr/gather | solution.py:52
  164.6 4.5 %constant_dynamic-slice_fusion.5 = s32[1,4,40,2048]{2,3,1,0:T(8,128)} fusion(s32[8,4,40,2048]{2,3,1,0:T(8,128)} %get-tuple-element.133, s32[]{:T(128)} %get-tuple-element.124), kind=kLoop, calls=%fused_computation.18.clone.1 | loop fusion | bytes 2621444 | tf_op jit(solution)/shard_map/while/body/jit(dynamic_index_in_dim)/dynamic_slice | solution.py:55
  172.7 6.2 %fusion.36 = f32[8,4,128,128]{3,2,1,0:T(8,128)} fusion(f32[8,4,128,128]{3,2,1,0:T(8,128)} %get-tuple-element.125, s32[]{:T(128)} %get-tuple-element.124, bf16[4,40,128,128]{3,2,1,0:T(8,128)(2,1)} %bitcast.61, s32[4,40]{1,0:T(4,128)S(1)} %fusion.35, s32[128]{0:T(128)S(1)} %shift_right_arithmetic.64, s32[4,40,128,16]{2,3,1,0:T(8,128)S(1)} %copy.20), kind=kOutput, calls=%fused_computation.12.clone.1 | convolution fusion | flops 681574400 | bytes 6817408 | tf_op jit(solution)/shard_map/while/body/eval_jaxpr/stij,stjf->sif/dot_general | solution.py:53
  179.7 11.2 %gather_fusion = bf16[160,128,128]{2,1,0:T(8,128)(2,1)} fusion(bf16[256,128,128]{2,1,0:T(8,128)(2,1)} %get-tuple-element.136, s32[1024]{0:T(1024)S(1)} %pad_clamp_fusion.2), kind=kCustom, calls=%fused_computation.clone.clone.1 | custom fusion | bytes 10486400 | tf_op jit(solution)/shard_map/while/body/eval_jaxpr/gather | solution.py:52
  190.9 4.5 %constant_dynamic-slice_fusion.5 = s32[1,4,40,2048]{2,3,1,0:T(8,128)} fusion(s32[8,4,40,2048]{2,3,1,0:T(8,128)} %get-tuple-element.133, s32[]{:T(128)} %get-tuple-element.124), kind=kLoop, calls=%fused_computation.18.clone.1 | loop fusion | bytes 2621444 | tf_op jit(solution)/shard_map/while/body/jit(dynamic_index_in_dim)/dynamic_slice | solution.py:55
  199.0 6.3 %fusion.36 = f32[8,4,128,128]{3,2,1,0:T(8,128)} fusion(f32[8,4,128,128]{3,2,1,0:T(8,128)} %get-tuple-element.125, s32[]{:T(128)} %get-tuple-element.124, bf16[4,40,128,128]{3,2,1,0:T(8,128)(2,1)} %bitcast.61, s32[4,40]{1,0:T(4,128)S(1)} %fusion.35, s32[128]{0:T(128)S(1)} %shift_right_arithmetic.64, s32[4,40,128,16]{2,3,1,0:T(8,128)S(1)} %copy.20), kind=kOutput, calls=%fused_computation.12.clone.1 | convolution fusion | flops 681574400 | bytes 6817408 | tf_op jit(solution)/shard_map/while/body/eval_jaxpr/stij,stjf->sif/dot_general | solution.py:53
  206.0 11.2 %gather_fusion = bf16[160,128,128]{2,1,0:T(8,128)(2,1)} fusion(bf16[256,128,128]{2,1,0:T(8,128)(2,1)} %get-tuple-element.136, s32[1024]{0:T(1024)S(1)} %pad_clamp_fusion.2), kind=kCustom, calls=%fused_computation.clone.clone.1 | custom fusion | bytes 10486400 | tf_op jit(solution)/shard_map/while/body/eval_jaxpr/gather | solution.py:52
  217.1 4.5 %constant_dynamic-slice_fusion.5 = s32[1,4,40,2048]{2,3,1,0:T(8,128)} fusion(s32[8,4,40,2048]{2,3,1,0:T(8,128)} %get-tuple-element.133, s32[]{:T(128)} %get-tuple-element.124), kind=kLoop, calls=%fused_computation.18.clone.1 | loop fusion | bytes 2621444 | tf_op jit(solution)/shard_map/while/body/jit(dynamic_index_in_dim)/dynamic_slice | solution.py:55
  225.2 6.3 %fusion.36 = f32[8,4,128,128]{3,2,1,0:T(8,128)} fusion(f32[8,4,128,128]{3,2,1,0:T(8,128)} %get-tuple-element.125, s32[]{:T(128)} %get-tuple-element.124, bf16[4,40,128,128]{3,2,1,0:T(8,128)(2,1)} %bitcast.61, s32[4,40]{1,0:T(4,128)S(1)} %fusion.35, s32[128]{0:T(128)S(1)} %shift_right_arithmetic.64, s32[4,40,128,16]{2,3,1,0:T(8,128)S(1)} %copy.20), kind=kOutput, calls=%fused_computation.12.clone.1 | convolution fusion | flops 681574400 | bytes 6817408 | tf_op jit(solution)/shard_map/while/body/eval_jaxpr/stij,stjf->sif/dot_general | solution.py:53
  232.3 11.2 %gather_fusion = bf16[160,128,128]{2,1,0:T(8,128)(2,1)} fusion(bf16[256,128,128]{2,1,0:T(8,128)(2,1)} %get-tuple-element.136, s32[1024]{0:T(1024)S(1)} %pad_clamp_fusion.2), kind=kCustom, calls=%fused_computation.clone.clone.1 | custom fusion | bytes 10486400 | tf_op jit(solution)/shard_map/while/body/eval_jaxpr/gather | solution.py:52
  243.4 4.5 %constant_dynamic-slice_fusion.5 = s32[1,4,40,2048]{2,3,1,0:T(8,128)} fusion(s32[8,4,40,2048]{2,3,1,0:T(8,128)} %get-tuple-element.133, s32[]{:T(128)} %get-tuple-element.124), kind=kLoop, calls=%fused_computation.18.clone.1 | loop fusion | bytes 2621444 | tf_op jit(solution)/shard_map/while/body/jit(dynamic_index_in_dim)/dynamic_slice | solution.py:55
  251.5 6.3 %fusion.36 = f32[8,4,128,128]{3,2,1,0:T(8,128)} fusion(f32[8,4,128,128]{3,2,1,0:T(8,128)} %get-tuple-element.125, s32[]{:T(128)} %get-tuple-element.124, bf16[4,40,128,128]{3,2,1,0:T(8,128)(2,1)} %bitcast.61, s32[4,40]{1,0:T(4,128)S(1)} %fusion.35, s32[128]{0:T(128)S(1)} %shift_right_arithmetic.64, s32[4,40,128,16]{2,3,1,0:T(8,128)S(1)} %copy.20), kind=kOutput, calls=%fused_computation.12.clone.1 | convolution fusion | flops 681574400 | bytes 6817408 | tf_op jit(solution)/shard_map/while/body/eval_jaxpr/stij,stjf->sif/dot_general | solution.py:53
  258.5 11.2 %gather_fusion = bf16[160,128,128]{2,1,0:T(8,128)(2,1)} fusion(bf16[256,128,128]{2,1,0:T(8,128)(2,1)} %get-tuple-element.136, s32[1024]{0:T(1024)S(1)} %pad_clamp_fusion.2), kind=kCustom, calls=%fused_computation.clone.clone.1 | custom fusion | bytes 10486400 | tf_op jit(solution)/shard_map/while/body/eval_jaxpr/gather | solution.py:52
  269.7 4.5 %constant_dynamic-slice_fusion.5 = s32[1,4,40,2048]{2,3,1,0:T(8,128)} fusion(s32[8,4,40,2048]{2,3,1,0:T(8,128)} %get-tuple-element.133, s32[]{:T(128)} %get-tuple-element.124), kind=kLoop, calls=%fused_computation.18.clone.1 | loop fusion | bytes 2621444 | tf_op jit(solution)/shard_map/while/body/jit(dynamic_index_in_dim)/dynamic_slice | solution.py:55
  277.8 6.3 %fusion.36 = f32[8,4,128,128]{3,2,1,0:T(8,128)} fusion(f32[8,4,128,128]{3,2,1,0:T(8,128)} %get-tuple-element.125, s32[]{:T(128)} %get-tuple-element.124, bf16[4,40,128,128]{3,2,1,0:T(8,128)(2,1)} %bitcast.61, s32[4,40]{1,0:T(4,128)S(1)} %fusion.35, s32[128]{0:T(128)S(1)} %shift_right_arithmetic.64, s32[4,40,128,16]{2,3,1,0:T(8,128)S(1)} %copy.20), kind=kOutput, calls=%fused_computation.12.clone.1 | convolution fusion | flops 681574400 | bytes 6817408 | tf_op jit(solution)/shard_map/while/body/eval_jaxpr/stij,stjf->sif/dot_general | solution.py:53
  284.8 11.2 %gather_fusion = bf16[160,128,128]{2,1,0:T(8,128)(2,1)} fusion(bf16[256,128,128]{2,1,0:T(8,128)(2,1)} %get-tuple-element.136, s32[1024]{0:T(1024)S(1)} %pad_clamp_fusion.2), kind=kCustom, calls=%fused_computation.clone.clone.1 | custom fusion | bytes 10486400 | tf_op jit(solution)/shard_map/while/body/eval_jaxpr/gather | solution.py:52
  296.0 4.5 %constant_dynamic-slice_fusion.5 = s32[1,4,40,2048]{2,3,1,0:T(8,128)} fusion(s32[8,4,40,2048]{2,3,1,0:T(8,128)} %get-tuple-element.133, s32[]{:T(128)} %get-tuple-element.124), kind=kLoop, calls=%fused_computation.18.clone.1 | loop fusion | bytes 2621444 | tf_op jit(solution)/shard_map/while/body/jit(dynamic_index_in_dim)/dynamic_slice | solution.py:55
  304.0 6.2 %fusion.36 = f32[8,4,128,128]{3,2,1,0:T(8,128)} fusion(f32[8,4,128,128]{3,2,1,0:T(8,128)} %get-tuple-element.125, s32[]{:T(128)} %get-tuple-element.124, bf16[4,40,128,128]{3,2,1,0:T(8,128)(2,1)} %bitcast.61, s32[4,40]{1,0:T(4,128)S(1)} %fusion.35, s32[128]{0:T(128)S(1)} %shift_right_arithmetic.64, s32[4,40,128,16]{2,3,1,0:T(8,128)S(1)} %copy.20), kind=kOutput, calls=%fused_computation.12.clone.1 | convolution fusion | flops 681574400 | bytes 6817408 | tf_op jit(solution)/shard_map/while/body/eval_jaxpr/stij,stjf->sif/dot_general | solution.py:53
  312.3 6.6 %maximum_convert_fusion = bf16[4096,512]{1,0:T(8,128)(2,1)} fusion(f32[4096,512]{1,0:T(8,128)} %fusion.21, bf16[4096,128]{1,0:T(8,128)(2,1)S(1)} %fusion.20, bf16[128,512]{1,0:T(8,128)(2,1)S(1)} %copy-done.4, f32[512]{0:T(512)S(1)} %copy-done.6), kind=kOutput, calls=%fused_computation.22 | convolution fusion | flops 545259520 | bytes 13764608 | tf_op jit(solution)/shard_map/dot_general | solution.py:67
  (98 shorter events, 47.4 us)
Async XLA Ops:
  6.5 4.2 %copy-start = (bf16[4096,128]{1,0:T(8,128)(2,1)S(1)}, bf16[4096,128]{1,0:T(8,128)(2,1)}, u32[]{:S(2)}) copy-start(bf16[4096,128]{1,0:T(8,128)(2,1)} %param.13) | copy-start | bytes 3145732
  6.5 86.2 %all-gather.4.cloned.1.call-start = ((), (), s32[]{:S(2)}) async-start(), calls=%async_computation | async-start | bytes 4325376 | tf_op jit(solution)/shard_map/all_gather | solution.py:34
  6.5 31.7 %collective-permute-start = (bf16[4096,128]{1,0:T(8,128)(2,1)}, bf16[4096,128]{1,0:T(8,128)(2,1)S(1)}, u32[]{:S(2)}, u32[]{:S(2)}) collective-permute-start(bf16[4096,128]{1,0:T(8,128)(2,1)} %param.12), channel_id=1, source_target_pairs={{0,3},{1,0},{2,1},{3,2},{4,7},{5,4},{6,5},{7,6},{8,11},{9,8},{10,9... | collective-permute-start | bytes 3145736 | tf_op jit(solution)/shard_map/ppermute | solution.py:28
  40.9 45.7 %collective-permute-start.1 = (bf16[8192,128]{1,0:T(8,128)(2,1)}, bf16[8192,128]{1,0:T(8,128)(2,1)}, u32[]{:S(2)}, u32[]{:S(2)}) collective-permute-start(bf16[8192,128]{1,0:T(8,128)(2,1)} %pad_maximum_fusion.1), channel_id=1, source_target_pairs={{0,2},{1,3},{2,0},{3,1},{4,6},{5,7},{6,4},{7,5},{8,10},{9,11},{10,... | collective-permute-start | bytes 6291464 | tf_op jit(solution)/shard_map/ppermute | solution.py:28
  42.2 20.5 %copy-start.7 = (s32[32]{0:T(128)S(1)}, s32[32]{0:T(128)}, u32[]{:S(2)}) copy-start(s32[32]{0:T(128)} %param.18) | copy-start | bytes 388
  42.2 20.5 %copy-start.5 = (s32[4096]{0:T(1024)S(1)}, s32[4096]{0:T(1024)}, u32[]{:S(2)}) copy-start(s32[4096]{0:T(1024)} %param.20) | copy-start | bytes 49156
  42.2 20.6 %copy-start.2 = (bf16[4096,128]{1,0:T(8,128)(2,1)S(1)}, bf16[4096,128]{1,0:T(8,128)(2,1)}, u32[]{:S(2)}) copy-start(bf16[4096,128]{1,0:T(8,128)(2,1)} %param.12) | copy-start | bytes 3145732
  42.2 20.6 %copy-start.3 = (bf16[128,512]{1,0:T(8,128)(2,1)S(1)}, bf16[128,512]{1,0:T(8,128)(2,1)}, u32[]{:S(2)}) copy-start(bf16[128,512]{1,0:T(8,128)(2,1)} %param.14) | copy-start | bytes 393220
  100.2 212.1 %copy-start.4 = (bf16[128,512]{1,0:T(8,128)(2,1)S(1)}, bf16[128,512]{1,0:T(8,128)(2,1)}, u32[]{:S(2)}) copy-start(bf16[128,512]{1,0:T(8,128)(2,1)} %param.15) | copy-start | bytes 393220
  100.2 212.2 %copy-start.6 = (f32[512]{0:T(512)S(1)}, f32[512]{0:T(512)}, u32[]{:S(2)}) copy-start(f32[512]{0:T(512)} %param.16) | copy-start | bytes 6148
  310.3 8.7 %copy-start.1 = (bf16[4096,128]{1,0:T(8,128)(2,1)S(1)}, bf16[4096,128]{1,0:T(8,128)(2,1)}, u32[]{:S(2)}) copy-start(bf16[4096,128]{1,0:T(8,128)(2,1)} %param.13) | copy-start | bytes 3145732
Sparse Core Ops, SparseCore 0:
  38.3 52.1 all-gather.3
